TPU v7x, 256 devices: a whole 4x4x8 slice. The times are simulated.
256 devices in a mesh: grp: 8 (over y, core), tp: 16 (over z, x_hi), sec: 2 (over x_lo).
Axes of the slice: x: 4 (x_hi: 2, x_lo: 2; x = x_hi * 2 + x_lo), y: 4, z: 8, core: 2. Of those that a mesh axis runs over, the one named last changes fastest.
Arguments:
- layer_in: bfloat16 [2, 512, 4, 8192], P('sec', 'grp', None, 'tp'), may hold values from -6 to 6
- q_weight: bfloat16 [2, 8192, 8192], P('sec', 'grp', 'tp'), may hold values from -0.0625 to 0.0625
- kv_weight: bfloat16 [2, 8192, 2048], P('sec', 'grp', 'tp'), may hold values from -0.0625 to 0.0625
- o_weight: bfloat16 [2, 8192, 8192], P('sec', 'tp', 'grp'), may hold values from -0.5 to 0.5
- kv_cache: bfloat16 [2, 512, 4096, 256], P('sec', 'grp', 'tp'), may hold values from -600 to 600
- cache_lengths: int32 [512], P('grp'), may hold values from 1 to 512, as said below
- value_head: float32 [8192], P('tp'), may hold values from -0.0625 to 0.0625
Outputs:
- hidden_out: bfloat16 [2, 512, 4, 8192], P('sec', 'grp', None, 'tp')
- token_gap: float32 [512, 4], P('grp', 'sec')
Inputs may be any that keep to these rules, and one draw needn't show every extreme that they name: `cache_lengths`: every rollout has at least one cached position; some rollout fills the whole cache and some holds a single position. Positions at or after a rollout's length hold arbitrary values.
All inputs are finite; a program needn't handle non-finite values.
Results may differ from a plain program's by a relative error of at most 0.018.
Values may be sent and summed in bfloat16 or wider, within the bound.
A program may use at most 128 MiB of HBM per device.

v0:
```python
import jax
import jax.numpy as jnp
from jax import lax
from jax.sharding import PartitionSpec as P

KVH = 8
HD = 128
CACHE = 512


def from_partner(value, axis, bit):
    mask = 2**bit
    pairs = [(source, source ^ mask) for source in range(lax.axis_size(axis))]
    return lax.ppermute(value, axis, pairs)


def local(layer_in, q_weight, kv_weight, o_weight, kv_cache, cache_lengths, value_head):
    tp_count = lax.axis_size("tp")
    tp_place = lax.axis_index("tp")
    sec_count = lax.axis_size("sec")
    sec_place = lax.axis_index("sec")
    rollouts = layer_in.shape[1]
    new_steps = layer_in.shape[2]
    tokens = rollouts * new_steps
    local_in = layer_in[0].reshape(tokens, layer_in.shape[3])
    full_in = lax.all_gather(local_in, "tp", axis=1, tiled=True)
    query_local = q_weight[0]
    pair_local = kv_weight[0]

    def add_rows(piece):
        return jnp.dot(full_in, piece, preferred_element_type=jnp.float32)

    query_sum = add_rows(lax.all_gather(query_local, "grp", axis=0, tiled=True))
    pair_sum = add_rows(lax.all_gather(pair_local, "grp", axis=0, tiled=True))
    query_vals = query_sum.astype(jnp.bfloat16)
    pair_vals = pair_sum.astype(jnp.bfloat16)
    pair_size = max(tp_count // KVH, 1)
    is_even = tp_place % 2 == 0
    query_other, pair_other = from_partner((query_vals, pair_vals), "tp", 0)
    query_low = jnp.where(is_even, query_vals, query_other)
    query_high = jnp.where(is_even, query_other, query_vals)
    query_all = jnp.concatenate([query_low, query_high], axis=1)
    local_heads = 1
    new_key = jnp.where(is_even, pair_vals, pair_other).reshape(rollouts, new_steps, 1, HD)
    new_value = jnp.where(is_even, pair_other, pair_vals).reshape(rollouts, new_steps, 1, HD)
    groups = query_all.shape[1] // (local_heads * HD)
    query_five = query_all.reshape(rollouts, new_steps, local_heads, groups, HD)
    rows_dev = kv_cache.shape[2]
    span = rows_dev // local_heads
    start_pos = tp_place * rows_dev % CACHE
    cache_five = kv_cache[0].reshape(rollouts, local_heads, span, 2, HD)
    cache_keys = cache_five[:, :, :, 0, :]
    cache_vals = cache_five[:, :, :, 1, :]
    leader = tp_place % pair_size == 0
    visible = ((start_pos + jnp.arange(span))[None, :] < cache_lengths[:, None])[
        :, None, None, None, :
    ]
    causal = (jnp.arange(new_steps)[None, :] <= jnp.arange(new_steps)[:, None]) & leader
    causal = causal[None, :, None, None, :]
    score_scale = HD ** (-0.5)
    cache_scores = (
        jnp.einsum("rskgd,rkpd->rskgp", query_five, cache_keys, preferred_element_type=jnp.float32)
        * score_scale
    )
    new_scores = (
        jnp.einsum("rskgd,rtkd->rskgt", query_five, new_key, preferred_element_type=jnp.float32)
        * score_scale
    )
    row_peak = jnp.maximum(
        jnp.max(jnp.where(visible, cache_scores, -1e30), axis=-1),
        jnp.max(jnp.where(causal, new_scores, -1e30), axis=-1),
    )
    cache_w = jnp.where(visible, jnp.exp(cache_scores - row_peak[..., None]), 0.0)
    new_w = jnp.where(causal, jnp.exp(new_scores - row_peak[..., None]), 0.0)
    row_total = jnp.sum(cache_w, axis=-1) + jnp.sum(new_w, axis=-1)
    weighted = jnp.einsum(
        "rskgp,rkpd->rskgd",
        cache_w.astype(jnp.bfloat16),
        cache_vals,
        preferred_element_type=jnp.float32,
    )
    weighted = weighted + jnp.einsum(
        "rskgt,rtkd->rskgd",
        new_w.astype(jnp.bfloat16),
        new_value,
        preferred_element_type=jnp.float32,
    )
    own_heads = groups // 2
    low_part = (
        row_peak[:, :, :, :own_heads],
        row_total[:, :, :, :own_heads],
        weighted[:, :, :, :own_heads],
    )
    high_part = (
        row_peak[:, :, :, own_heads:],
        row_total[:, :, :, own_heads:],
        weighted[:, :, :, own_heads:],
    )
    send_part = tuple(
        (jnp.where(is_even, high_one, low_one) for low_one, high_one in zip(low_part, high_part))
    )
    keep_part = tuple(
        (jnp.where(is_even, low_one, high_one) for low_one, high_one in zip(low_part, high_part))
    )
    got_part = (
        from_partner(send_part[0].astype(jnp.bfloat16), "tp", 0).astype(jnp.float32),
        from_partner(send_part[1].astype(jnp.bfloat16), "tp", 0).astype(jnp.float32),
        from_partner(send_part[2].astype(jnp.bfloat16), "tp", 0).astype(jnp.float32),
    )
    merged_peak = jnp.maximum(keep_part[0], got_part[0])
    own_factor = jnp.exp(keep_part[0] - merged_peak)
    far_factor = jnp.exp(got_part[0] - merged_peak)
    row_total = keep_part[1] * own_factor + got_part[1] * far_factor
    weighted = keep_part[2] * own_factor[..., None] + got_part[2] * far_factor[..., None]
    context = (weighted / row_total[..., None]).astype(jnp.bfloat16).reshape(tokens, -1)
    head_terms = jnp.dot(
        context,
        lax.all_gather(o_weight[0], "grp", axis=1, tiled=True),
        preferred_element_type=jnp.float32,
    )
    result = lax.psum_scatter(
        head_terms.astype(jnp.bfloat16), "tp", scatter_dimension=1, tiled=True
    )
    other_result = from_partner(result, "sec", 0)
    policy_part = jnp.where(sec_place == 0, result, other_result).astype(jnp.float32)
    refer_part = jnp.where(sec_place == 0, other_result, result).astype(jnp.float32)
    local_gap = jnp.sum((policy_part - refer_part) * value_head, axis=1)
    token_gap = lax.psum(local_gap, "tp")
    hidden_out = result.reshape(1, rollouts, new_steps, result.shape[1])
    gap_grid = token_gap.reshape(rollouts, new_steps)
    step_share = new_steps // sec_count
    own_gap = lax.dynamic_slice_in_dim(gap_grid, sec_place * step_share, step_share, 1)
    return (hidden_out, own_gap)


def solution(mesh):
    placed = (
        P("sec", "grp", None, "tp"),
        P("sec", "grp", "tp"),
        P("sec", "grp", "tp"),
        P("sec", "tp", "grp"),
        P("sec", "grp", "tp", None),
        P("grp"),
        P("tp"),
    )
    return jax.shard_map(
        local,
        mesh=mesh,
        in_specs=placed,
        out_specs=(P("sec", "grp", None, "tp"), P("grp", "sec")),
        check_vma=False,
    )
```

profile of v0, /device:TPU:8, one launch (start us, length us, event | category | flops | bytes accessed | tf_op | source)
XLA Modules:
  0.0 563.6 jit_solution(2793352173244113551)
XLA Ops:
  7.2 0.7 all-gather.12.cloned.1.call-update
  7.9 1.7 reshape_squeeze.6
  9.7 0.7 all-gather.10.cloned.1.call-update
  10.5 0.5 all-gather.14.cloned.1.call-update
  11.1 0.7 broadcast_compare_fusion
  11.8 27.7 %all-gather.12.cloned.1.call-done = bf16[1,8192,128]{2,1,0:T(8,128)(2,1)} async-done(((bf16[1,1024,128]{2,1,0:T(8,128)(2,1)}), bf16[1,8192,128]{2,1,0:T(8,128)(2,1)}) %all-gather.12.cloned.1.call-update) | async-done | bytes 2097168 | tf_op jit(solution)/shard_map/all_gather | solution.py:34
  39.6 109.6 %all-gather.8.cloned.1.call-done = bf16[256,8192]{1,0:T(8,128)(2,1)} async-done(((bf16[256,512]{1,0:T(8,128)(2,1)}), bf16[256,8192]{1,0:T(8,128)(2,1)}) %all-gather.8.cloned.1.call-update) | async-done | bytes 4194320 | tf_op jit(solution)/shard_map/all_gather | solution.py:26
  149.2 4.1 fusion.16
  153.3 0.6 collective-permute-start.1
  154.0 45.2 %all-gather.10.cloned.1.call-done = bf16[1,8192,512]{2,1,0:T(8,128)(2,1)} async-done(((bf16[1,1024,512]{2,1,0:T(8,128)(2,1)}), bf16[1,8192,512]{2,1,0:T(8,128)(2,1)}) %all-gather.10.cloned.1.call-update) | async-done | bytes 8388624 | tf_op jit(solution)/shard_map/all_gather | solution.py:33
  199.1 7.0 %fusion.13 = bf16[256,512]{1,0:T(8,128)(2,1)S(1)} fusion(bf16[256,8192]{1,0:T(8,128)(2,1)} %all-gather.8.cloned.1.call-done, bf16[1,8192,512]{2,1,0:T(8,128)(2,1)} %all-gather.10.cloned.1.call-done), kind=kOutput, calls=%fused_computation.22 | convolution fusion | flops 2147614720 | bytes 12845056 | tf_op jit(solution)/shard_map/dot_general | solution.py:31
  206.1 3.1 collective-permute-start
  209.2 11.7 %copy.9 = bf16[1,64,256,256]{2,3,1,0:T(8,128)(2,1)} copy(bf16[1,64,256,256]{3,2,1,0:T(8,128)(2,1)} %param.11) | data formatting | bytes 16777216 | tf_op args[4]
  221.1 2.4 select_reduce_fusion
  223.6 3.3 fusion.7
  227.0 0.5 fusion.26
  227.5 0.9 bitcast_reduce_fusion
  228.5 0.9 collective-permute-start.4
  229.6 2.8 collective-permute-start.2
  232.4 1.6 fusion.10
  234.7 1.1 collective-permute-start.3
  236.2 8.3 %collective-permute-done.3 = bf16[64,4,1,4,128]{4,3,1,0,2:T(4,128)(2,1)S(1)} collective-permute-done((bf16[64,4,1,4,128]{4,3,1,0,2:T(4,128)(2,1)S(1)}, bf16[64,4,1,4,128]{4,3,1,0,2:T(4,128)(2,1)S(1)}, u32[]{:S(2)}, u32[]{:S(2)}) %collective-permute-start.3) | collective-permute-done | bytes 262176 | tf_op jit(solution)/shard_map/ppermute | solution.py:14
  244.5 1.0 fusion.25
  245.4 7.9 %all-gather.14.cloned.1.call-done = bf16[1,512,8192]{2,1,0:T(8,128)(2,1)} async-done(((bf16[1,512,1024]{2,1,0:T(8,128)(2,1)}), bf16[1,512,8192]{2,1,0:T(8,128)(2,1)}) %all-gather.14.cloned.1.call-update) | async-done | bytes 8388624 | tf_op jit(solution)/shard_map/all_gather | solution.py:118
  253.3 7.7 %convolution_convert_fusion = bf16[256,8192]{1,0:T(8,128)(2,1)} fusion(bf16[1,512,8192]{2,1,0:T(8,128)(2,1)} %all-gather.14.cloned.1.call-done, bf16[32,8,4,128]{3,2,1,0:T(4,128)(2,1)S(1)} %bitcast.117), kind=kOutput, calls=%fused_computation | convolution fusion | flops 2149580800 | bytes 12845056 | tf_op jit(solution)/shard_map/dot_general | solution.py:116
  261.1 213.8 %reduce-scatter.2.cloned.1.call-done = bf16[256,512]{1,0:T(8,128)(2,1)} async-done(((bf16[256,8192]{1,0:T(8,128)(2,1)}), bf16[256,512]{1,0:T(8,128)(2,1)}) %reduce-scatter.2.cloned.1.call-update) | async-done | bytes 262160 | tf_op jit(solution)/shard_map/reduce_scatter | solution.py:121
  474.9 0.5 collective-permute-start.5
  475.4 1.8 reshape.158
  477.2 4.3 collective-permute-done.5
  481.5 1.1 multiply_reduce_fusion
  482.7 73.6 %psum.7 = f32[64,4]{1,0:T(8,128)S(1)} all-reduce(f32[64,4]{1,0:T(8,128)S(1)} %reshape.159), channel_id=1, replica_groups=mesh['grp'=8,'tp'=16,'sec'=2] {'tp'}, use_global_device_ids=true, to_apply=%region_6.7 | all-reduce | flops 256 | bytes 2048 | tf_op jit(solution)/shard_map/psum | solution.py:128
  556.4 0.6 copy.12
  (34 shorter events, 2.0 us)
Async XLA Ops:
  7.2 32.4 %all-gather.12.cloned.1.call-start = ((), (), s32[]{:S(2)}) async-start(), calls=%async_computation.4 | async-start | bytes 2359296 | tf_op jit(solution)/shard_map/all_gather | solution.py:34
  7.9 141.3 %all-gather.8.cloned.1.call-start = ((), (), s32[]{:S(2)}) async-start(), calls=%async_computation.1 | async-start | bytes 4456448 | tf_op jit(solution)/shard_map/all_gather | solution.py:26
  9.7 189.4 %all-gather.10.cloned.1.call-start = ((), (), s32[]{:S(2)}) async-start(), calls=%async_computation.3 | async-start | bytes 9437184 | tf_op jit(solution)/shard_map/all_gather | solution.py:33
  10.4 242.9 %all-gather.14.cloned.1.call-start = ((), (), s32[]{:S(2)}) async-start(), calls=%async_computation.5 | async-start | bytes 9437184 | tf_op jit(solution)/shard_map/all_gather | solution.py:118
  11.0 463.9 %reduce-scatter.2.cloned.1.call-start = ((), (), s32[]{:S(2)}) async-start(), calls=%async_computation.2 | async-start | bytes 4456448 | tf_op jit(solution)/shard_map/reduce_scatter | solution.py:121
  153.3 67.6 %collective-permute-start.1 = (bf16[256,128]{1,0:T(8,128)(2,1)S(1)}, bf16[256,128]{1,0:T(8,128)(2,1)S(1)}, u32[]{:S(2)}, u32[]{:S(2)}) collective-permute-start(bf16[256,128]{1,0:T(8,128)(2,1)S(1)} %fusion.16), channel_id=1, source_target_pairs={{0,2},{2,0},{4,6},{6,4},{8,10},{10,8},{12,14},{14,12},{16,18},{18,... | collective-permute-start | bytes 196616 | tf_op jit(solution)/shard_map/ppermute | solution.py:14
  206.1 14.8 %collective-permute-start = (bf16[256,512]{1,0:T(8,128)(2,1)S(1)}, bf16[256,512]{1,0:T(8,128)(2,1)S(1)}, u32[]{:S(2)}, u32[]{:S(2)}) collective-permute-start(bf16[256,512]{1,0:T(8,128)(2,1)S(1)} %fusion.13), channel_id=1, source_target_pairs={{0,2},{2,0},{4,6},{6,4},{8,10},{10,8},{12,14},{14,12},{16,18},{18,... | collective-permute-start | bytes 786440 | tf_op jit(solution)/shard_map/ppermute | solution.py:14
  220.9 11.5 %slice-start = ((s8[8388608]{0:T(1024)(128)(4,1)}), s8[4194304]{0:T(1024)(128)(4,1)S(1)}, s32[]{:S(2)}) async-start(s8[8388608]{0:T(1024)(128)(4,1)} %bitcast.110), calls=%async_computation.6 | async-start | bytes 8388608
  223.6 8.8 %slice-start.1 = ((s8[8388608]{0:T(1024)(128)(4,1)}), s8[4194304]{0:T(1024)(128)(4,1)S(1)}, s32[]{:S(2)}) async-start(s8[8388608]{0:T(1024)(128)(4,1)} %bitcast.110), calls=%async_computation.7 | async-start | bytes 8388608
  228.5 7.5 %collective-permute-start.4 = (bf16[64,4,1,4]{3,1,0,2:T(4,128)(2,1)S(1)}, bf16[64,4,1,4]{3,1,0,2:T(4,128)(2,1)S(1)}, u32[]{:S(2)}, u32[]{:S(2)}) collective-permute-start(bf16[64,4,1,4]{3,1,0,2:T(4,128)(2,1)S(1)} %select_convert_fusion.1), channel_id=1, source_target_pairs={{0,2},{2,0},{4,6},{6,4},{8,10},{10,8},{12,14},{14,12},{16,18},{18,... | collective-permute-start | bytes 6152 | tf_op jit(solution)/shard_map/ppermute | solution.py:14
  229.6 6.3 %collective-permute-start.2 = (bf16[64,4,1,4]{3,1,0,2:T(4,128)(2,1)S(1)}, bf16[64,4,1,4]{3,1,0,2:T(4,128)(2,1)S(1)}, u32[]{:S(2)}, u32[]{:S(2)}) collective-permute-start(bf16[64,4,1,4]{3,1,0,2:T(4,128)(2,1)S(1)} %select_convert_fusion.2), channel_id=1, source_target_pairs={{0,2},{2,0},{4,6},{6,4},{8,10},{10,8},{12,14},{14,12},{16,18},{18,... | collective-permute-start | bytes 6152 | tf_op jit(solution)/shard_map/ppermute | solution.py:14
  234.7 9.8 %collective-permute-start.3 = (bf16[64,4,1,4,128]{4,3,1,0,2:T(4,128)(2,1)S(1)}, bf16[64,4,1,4,128]{4,3,1,0,2:T(4,128)(2,1)S(1)}, u32[]{:S(2)}, u32[]{:S(2)}) collective-permute-start(bf16[64,4,1,4,128]{4,3,1,0,2:T(4,128)(2,1)S(1)} %select_convert_fusion), channel_id=1, source_target_pairs={{0,2},{2,0},{4,6},{6,4},{8,10},{10,8},{12,14},{14,12},{16,18},{18,... | collective-permute-start | bytes 786440 | tf_op jit(solution)/shard_map/ppermute | solution.py:14
  261.0 220.4 %copy-start = (f32[512]{0:T(512)S(1)}, f32[512]{0:T(512)}, u32[]{:S(2)}) copy-start(f32[512]{0:T(512)} %param.13) | copy-start | bytes 6148
  474.9 6.6 %collective-permute-start.5 = (bf16[256,512]{1,0:T(8,128)(2,1)}, bf16[256,512]{1,0:T(8,128)(2,1)S(1)}, u32[]{:S(2)}, u32[]{:S(2)}) collective-permute-start(bf16[256,512]{1,0:T(8,128)(2,1)} %reduce-scatter.2.cloned.1.call-done), channel_id=1, source_target_pairs={{0,1},{1,0},{2,3},{3,2},{4,5},{5,4},{6,7},{7,6},{8,9},{9,8},{10,11... | collective-permute-start | bytes 786440 | tf_op jit(solution)/shard_map/ppermute | solution.py:14
Sparse Core Ops, SparseCore 0:
  9.9 29.6 all-gather.11
  42.6 106.5 all-gather.7
  151.1 48.0 all-gather.9
  200.8 52.4 all-gather.13
  261.2 213.6 reduce-scatter.1
where the time goes:
time: 564 us
  waiting for transfers between devices  419 us (74%)
  blocking collectives  73.6 us (13%)
  matrix products  26.7 us (5%)
  local copies, waits for them, and re-layouts  16.1 us (3%)
  between operations  14 us (2%)
  starting transfers between devices  9.26 us (2%)
    reduce_scatter x1, waiting for transfers between devices, local(): lax.psum_scatter(head_terms.astype(jnp.bfloat16), 'tp', scatter_dimension...  214 us
    all_gather x1, waiting for transfers between devices, local(): full_in = lax.all_gather(local_in, 'tp', axis=1, tiled=True)  110 us
    psum x1, blocking collectives, local(): token_gap = lax.psum(local_gap, 'tp')  73.6 us
    all_gather x1, waiting for transfers between devices, local(): query_sum = add_rows(lax.all_gather(query_local, 'grp', axis=0, tiled=True))  45.2 us
    all_gather x1, waiting for transfers between devices, local(): pair_sum = add_rows(lax.all_gather(pair_local, 'grp', axis=0, tiled=True))  27.7 us
    ppermute x6, waiting for transfers between devices, from_partner(): return lax.ppermute(value, axis, pairs)  12.6 us
    unnamed x9, local copies, waits for them, and re-layouts  12.4 us
  transfers between devices with their start and end apart: 11, of which 8 were waited for; matrix products, arithmetic and copies ran while one was open for 7% of the time, Pallas kernels for 0%

commit v1 on v0

--- a/solution.py
+++ b/solution.py
@@ -31,7 +31,11 @@
         return jnp.dot(full_in, piece, preferred_element_type=jnp.float32)
 
     query_sum = add_rows(lax.all_gather(query_local, "grp", axis=0, tiled=True))
-    pair_sum = add_rows(lax.all_gather(pair_local, "grp", axis=0, tiled=True))
+    pair_sum = add_rows(
+        jnp.concatenate(
+            lax.all_to_all(jnp.stack([pair_local] * lax.axis_size("grp")), "grp", 0, 0), axis=0
+        )
+    )
     query_vals = query_sum.astype(jnp.bfloat16)
     pair_vals = pair_sum.astype(jnp.bfloat16)
     pair_size = max(tp_count // KVH, 1)

time: 564 us -> 534 us (0.947)
  waiting for transfers between devices: 419 us -> 382 us
    all_gather x1, waiting for transfers between devices: 110 us -> 74.9 us  [local(): full_in = lax.all_gather(local_in, 'tp', axis=1, tiled=True)]
    all_gather x1 -> x0, waiting for transfers between devices: 27.7 us -> none  [local(): pair_sum = add_rows(lax.all_gather(pair_local, 'grp', axis=0, tiled=True))]
    all_to_all x0 -> x1, waiting for transfers between devices: none -> 25.7 us  [local(): lax.all_to_all(jnp.stack([pair_local] * lax.axis_size('grp')), 'grp', 0, 0)]
    all_to_all x0 -> x1, starting transfers between devices: none -> 5.7 us  [local(): lax.all_to_all(jnp.stack([pair_local] * lax.axis_size('grp')), 'grp', 0, 0)]
    unnamed x9 -> x11, local copies, waits for them, and re-layouts: 12.4 us -> 12.8 us
where the time goes in v1:
time: 534 us
  waiting for transfers between devices  382 us (72%)
  blocking collectives  73.5 us (14%)
  matrix products  26 us (5%)
  local copies, waits for them, and re-layouts  18.9 us (4%)
  starting transfers between devices  14.6 us (3%)
  between operations  14 us (3%)
    reduce_scatter x1, waiting for transfers between devices, local(): lax.psum_scatter(head_terms.astype(jnp.bfloat16), 'tp', scatter_dimension...  214 us
    all_gather x1, waiting for transfers between devices, local(): full_in = lax.all_gather(local_in, 'tp', axis=1, tiled=True)  74.9 us
    psum x1, blocking collectives, local(): token_gap = lax.psum(local_gap, 'tp')  73.5 us
    all_gather x1, waiting for transfers between devices, local(): query_sum = add_rows(lax.all_gather(query_local, 'grp', axis=0, tiled=True))  45.8 us
    all_to_all x1, waiting for transfers between devices, local(): lax.all_to_all(jnp.stack([pair_local] * lax.axis_size('grp')), 'grp', 0, 0)  25.7 us
    unnamed x11, local copies, waits for them, and re-layouts  12.8 us
    ppermute x6, waiting for transfers between devices, from_partner(): return lax.ppermute(value, axis, pairs)  12.7 us
  transfers between devices with their start and end apart: 11, of which 8 were waited for; matrix products, arithmetic and copies ran while one was open for 7% of the time, Pallas kernels for 0%

profile of v1, /device:TPU:8, one launch (start us, length us, event | category | flops | bytes accessed | tf_op | source)
XLA Modules:
  0.0 533.8 jit_solution(4088650251006069198)
XLA Ops:
  7.2 1.7 reshape_squeeze.6
  9.0 0.7 all-gather.8.cloned.1.call-update
  9.8 0.7 all-gather.10.cloned.1.call-update
  10.5 2.5 stack.3
  13.0 5.7 %all-to-all-start = ((bf16[8,1024,128]{2,1,0:T(8,128)(2,1)}), bf16[8,1024,128]{2,1,0:T(8,128)(2,1)S(1)}, u32[]{:S(2)}, u32[]{:S(2)}) async-start(bf16[8,1024,128]{2,1,0:T(8,128)(2,1)} %stack.3), calls=%async_computation | async-start | bytes 4194304 | tf_op jit(solution)/shard_map/all_to_all | solution.py:36
  18.8 25.7 %all-to-all-done = bf16[8,1024,128]{2,1,0:T(8,128)(2,1)S(1)} async-done(((bf16[8,1024,128]{2,1,0:T(8,128)(2,1)}), bf16[8,1024,128]{2,1,0:T(8,128)(2,1)S(1)}, u32[]{:S(2)}, u32[]{:S(2)}) %all-to-all-start) | async-done | bytes 2097184 | tf_op jit(solution)/shard_map/all_to_all | solution.py:36
  44.5 74.9 %all-gather.6.cloned.1.call-done = bf16[256,8192]{1,0:T(8,128)(2,1)} async-done(((bf16[256,512]{1,0:T(8,128)(2,1)}), bf16[256,8192]{1,0:T(8,128)(2,1)}) %all-gather.6.cloned.1.call-update) | async-done | bytes 4194320 | tf_op jit(solution)/shard_map/all_gather | solution.py:26
  119.4 3.4 convolution_convert_fusion.1
  122.8 0.6 collective-permute-start.1
  123.5 45.8 %all-gather.8.cloned.1.call-done = bf16[1,8192,512]{2,1,0:T(8,128)(2,1)} async-done(((bf16[1,1024,512]{2,1,0:T(8,128)(2,1)}), bf16[1,8192,512]{2,1,0:T(8,128)(2,1)}) %all-gather.8.cloned.1.call-update) | async-done | bytes 8388624 | tf_op jit(solution)/shard_map/all_gather | solution.py:33
  169.3 7.0 %fusion.11 = bf16[256,512]{1,0:T(8,128)(2,1)S(1)} fusion(bf16[256,8192]{1,0:T(8,128)(2,1)} %all-gather.6.cloned.1.call-done, bf16[1,8192,512]{2,1,0:T(8,128)(2,1)} %all-gather.8.cloned.1.call-done), kind=kOutput, calls=%fused_computation.20 | convolution fusion | flops 2147614720 | bytes 12845056 | tf_op jit(solution)/shard_map/dot_general | solution.py:31
  176.3 3.1 collective-permute-start
  179.4 12.0 %copy.9 = bf16[1,64,256,256]{2,3,1,0:T(8,128)(2,1)} copy(bf16[1,64,256,256]{3,2,1,0:T(8,128)(2,1)} %param.11) | data formatting | bytes 16777216 | tf_op args[4]
  191.6 2.4 select_reduce_fusion
  194.1 3.3 fusion.5
  197.5 0.5 fusion.21
  198.0 0.9 bitcast_reduce_fusion
  199.0 0.6 collective-permute-start.4
  199.8 3.1 collective-permute-start.2
  202.9 1.6 fusion.8
  205.2 0.8 collective-permute-start.3
  206.4 8.3 %collective-permute-done.3 = bf16[64,4,1,4,128]{4,3,1,0,2:T(4,128)(2,1)S(1)} collective-permute-done((bf16[64,4,1,4,128]{4,3,1,0,2:T(4,128)(2,1)S(1)}, bf16[64,4,1,4,128]{4,3,1,0,2:T(4,128)(2,1)S(1)}, u32[]{:S(2)}, u32[]{:S(2)}) %collective-permute-start.3) | collective-permute-done | bytes 262176 | tf_op jit(solution)/shard_map/ppermute | solution.py:14
  214.7 1.0 fusion.20
  215.6 8.0 %all-gather.10.cloned.1.call-done = bf16[1,512,8192]{2,1,0:T(8,128)(2,1)} async-done(((bf16[1,512,1024]{2,1,0:T(8,128)(2,1)}), bf16[1,512,8192]{2,1,0:T(8,128)(2,1)}) %all-gather.10.cloned.1.call-update) | async-done | bytes 8388624 | tf_op jit(solution)/shard_map/all_gather | solution.py:122
  223.7 7.7 %convolution_convert_fusion = bf16[256,8192]{1,0:T(8,128)(2,1)} fusion(bf16[1,512,8192]{2,1,0:T(8,128)(2,1)} %all-gather.10.cloned.1.call-done, bf16[32,8,4,128]{3,2,1,0:T(4,128)(2,1)S(1)} %bitcast.117), kind=kOutput, calls=%fused_computation | convolution fusion | flops 2149580800 | bytes 12845056 | tf_op jit(solution)/shard_map/dot_general | solution.py:120
  231.4 213.8 %reduce-scatter.2.cloned.1.call-done = bf16[256,512]{1,0:T(8,128)(2,1)} async-done(((bf16[256,8192]{1,0:T(8,128)(2,1)}), bf16[256,512]{1,0:T(8,128)(2,1)}) %reduce-scatter.2.cloned.1.call-update) | async-done | bytes 262160 | tf_op jit(solution)/shard_map/reduce_scatter | solution.py:125
  445.2 0.5 collective-permute-start.5
  445.7 1.8 reshape.163
  447.5 4.3 collective-permute-done.5
  451.8 1.1 multiply_reduce_fusion
  453.0 73.5 %psum.7 = f32[64,4]{1,0:T(8,128)S(1)} all-reduce(f32[64,4]{1,0:T(8,128)S(1)} %reshape.164), channel_id=1, replica_groups=mesh['grp'=8,'tp'=16,'sec'=2] {'tp'}, use_global_device_ids=true, to_apply=%region_6.7 | all-reduce | flops 256 | bytes 2048 | tf_op jit(solution)/shard_map/psum | solution.py:132
  526.6 0.6 copy.12
  (36 shorter events, 2.0 us)
Async XLA Ops:
  7.2 112.2 %all-gather.6.cloned.1.call-start = ((), (), s32[]{:S(2)}) async-start(), calls=%async_computation.2 | async-start | bytes 4456448 | tf_op jit(solution)/shard_map/all_gather | solution.py:26
  9.0 9.8 %copy-start.1 = (s32[64]{0:T(128)S(1)}, s32[64]{0:T(128)}, u32[]{:S(2)}) copy-start(s32[64]{0:T(128)} %param.12) | copy-start | bytes 772
  9.0 160.3 %all-gather.8.cloned.1.call-start = ((), (), s32[]{:S(2)}) async-start(), calls=%async_computation.4 | async-start | bytes 9437184 | tf_op jit(solution)/shard_map/all_gather | solution.py:33
  9.7 214.0 %all-gather.10.cloned.1.call-start = ((), (), s32[]{:S(2)}) async-start(), calls=%async_computation.5 | async-start | bytes 9437184 | tf_op jit(solution)/shard_map/all_gather | solution.py:122
  13.0 31.5 %all-to-all-start = ((bf16[8,1024,128]{2,1,0:T(8,128)(2,1)}), bf16[8,1024,128]{2,1,0:T(8,128)(2,1)S(1)}, u32[]{:S(2)}, u32[]{:S(2)}) async-start(bf16[8,1024,128]{2,1,0:T(8,128)(2,1)} %stack.3), calls=%async_computation | async-start | bytes 4194304 | tf_op jit(solution)/shard_map/all_to_all | solution.py:36
  18.7 426.5 %reduce-scatter.2.cloned.1.call-start = ((), (), s32[]{:S(2)}) async-start(), calls=%async_computation.3 | async-start | bytes 4456448 | tf_op jit(solution)/shard_map/reduce_scatter | solution.py:125
  122.8 68.5 %collective-permute-start.1 = (bf16[256,128]{1,0:T(8,128)(2,1)S(1)}, bf16[256,128]{1,0:T(8,128)(2,1)S(1)}, u32[]{:S(2)}, u32[]{:S(2)}) collective-permute-start(bf16[256,128]{1,0:T(8,128)(2,1)S(1)} %convolution_convert_fusion.1), channel_id=1, source_target_pairs={{0,2},{2,0},{4,6},{6,4},{8,10},{10,8},{12,14},{14,12},{16,18},{18,... | collective-permute-start | bytes 196616 | tf_op jit(solution)/shard_map/ppermute | solution.py:14
  176.3 15.1 %collective-permute-start = (bf16[256,512]{1,0:T(8,128)(2,1)S(1)}, bf16[256,512]{1,0:T(8,128)(2,1)S(1)}, u32[]{:S(2)}, u32[]{:S(2)}) collective-permute-start(bf16[256,512]{1,0:T(8,128)(2,1)S(1)} %fusion.11), channel_id=1, source_target_pairs={{0,2},{2,0},{4,6},{6,4},{8,10},{10,8},{12,14},{14,12},{16,18},{18,... | collective-permute-start | bytes 786440 | tf_op jit(solution)/shard_map/ppermute | solution.py:14
  191.4 11.5 %slice-start = ((s8[8388608]{0:T(1024)(128)(4,1)}), s8[4194304]{0:T(1024)(128)(4,1)S(1)}, s32[]{:S(2)}) async-start(s8[8388608]{0:T(1024)(128)(4,1)} %bitcast.108), calls=%async_computation.6 | async-start | bytes 8388608
  194.1 8.8 %slice-start.1 = ((s8[8388608]{0:T(1024)(128)(4,1)}), s8[4194304]{0:T(1024)(128)(4,1)S(1)}, s32[]{:S(2)}) async-start(s8[8388608]{0:T(1024)(128)(4,1)} %bitcast.108), calls=%async_computation.7 | async-start | bytes 8388608
  199.0 7.2 %collective-permute-start.4 = (bf16[64,4,1,4]{3,1,0,2:T(4,128)(2,1)S(1)}, bf16[64,4,1,4]{3,1,0,2:T(4,128)(2,1)S(1)}, u32[]{:S(2)}, u32[]{:S(2)}) collective-permute-start(bf16[64,4,1,4]{3,1,0,2:T(4,128)(2,1)S(1)} %select_convert_fusion.1), channel_id=1, source_target_pairs={{0,2},{2,0},{4,6},{6,4},{8,10},{10,8},{12,14},{14,12},{16,18},{18,... | collective-permute-start | bytes 6152 | tf_op jit(solution)/shard_map/ppermute | solution.py:14
  199.8 6.3 %collective-permute-start.2 = (bf16[64,4,1,4]{3,1,0,2:T(4,128)(2,1)S(1)}, bf16[64,4,1,4]{3,1,0,2:T(4,128)(2,1)S(1)}, u32[]{:S(2)}, u32[]{:S(2)}) collective-permute-start(bf16[64,4,1,4]{3,1,0,2:T(4,128)(2,1)S(1)} %select_convert_fusion.2), channel_id=1, source_target_pairs={{0,2},{2,0},{4,6},{6,4},{8,10},{10,8},{12,14},{14,12},{16,18},{18,... | collective-permute-start | bytes 6152 | tf_op jit(solution)/shard_map/ppermute | solution.py:14
  205.2 9.5 %collective-permute-start.3 = (bf16[64,4,1,4,128]{4,3,1,0,2:T(4,128)(2,1)S(1)}, bf16[64,4,1,4,128]{4,3,1,0,2:T(4,128)(2,1)S(1)}, u32[]{:S(2)}, u32[]{:S(2)}) collective-permute-start(bf16[64,4,1,4,128]{4,3,1,0,2:T(4,128)(2,1)S(1)} %select_convert_fusion), channel_id=1, source_target_pairs={{0,2},{2,0},{4,6},{6,4},{8,10},{10,8},{12,14},{14,12},{16,18},{18,... | collective-permute-start | bytes 786440 | tf_op jit(solution)/shard_map/ppermute | solution.py:14
  231.4 220.4 %copy-start = (f32[512]{0:T(512)S(1)}, f32[512]{0:T(512)}, u32[]{:S(2)}) copy-start(f32[512]{0:T(512)} %param.13) | copy-start | bytes 6148
  445.2 6.6 %collective-permute-start.5 = (bf16[256,512]{1,0:T(8,128)(2,1)}, bf16[256,512]{1,0:T(8,128)(2,1)S(1)}, u32[]{:S(2)}, u32[]{:S(2)}) collective-permute-start(bf16[256,512]{1,0:T(8,128)(2,1)} %reduce-scatter.2.cloned.1.call-done), channel_id=1, source_target_pairs={{0,1},{1,0},{2,3},{3,2},{4,5},{5,4},{6,7},{7,6},{8,9},{9,8},{10,11... | collective-permute-start | bytes 786440 | tf_op jit(solution)/shard_map/ppermute | solution.py:14
Sparse Core Ops, SparseCore 0:
  11.0 108.3 all-gather.5
  121.3 48.0 all-gather.7
  171.2 52.4 all-gather.9
  231.5 213.6 reduce-scatter.1
